TPU v7x, 32 devices: a whole 2x2x4 slice. The times are simulated.
32 devices in a mesh: grp: 2 (over y), mp: 16 (over z, x, core).
Axes of the slice: x: 2, y: 2, z: 4, core: 2. Of those that a mesh axis runs over, the one named last changes fastest.
Arguments:
- query_grad: bfloat16 [64, 8192], P('grp'), parts along dimension 0, may hold values from -0.0625 to 0.0625
- query_input: bfloat16 [64, 8192], P('grp'), parts along dimension 0, may hold values from -6 to 6
- query_ids: int32 [64], P('grp'), parts along dimension 0, may hold values from 0 to 7, never falling along the last dimension, each value on 1 to 8 neighbouring positions
- train_grad: bfloat16 [256, 8192], P('grp'), parts along dimension 0, may hold values from -0.0625 to 0.0625
- train_input: bfloat16 [256, 8192], P('grp'), parts along dimension 0, may hold values from -3 to 3
- train_ids: int32 [256], P('grp'), parts along dimension 0, may hold values from 0 to 15, never falling along the last dimension, each value on 1 to 16 neighbouring positions
- output_basis: bfloat16 [8192, 8192], P(None, 'mp'), may hold values from -0.0625 to 0.0625
- input_basis: bfloat16 [8192, 8192], P(None, 'mp'), may hold values from -0.0625 to 0.0625
- eigenvalues: float32 [8192, 8192], P('mp'), may hold values from 0.05 to 5
Outputs:
- scores: float32 [16, 16], P('grp'), parts along dimension 0
There are 2 independent parts, one for each index of `grp`. A program takes and returns all parts, laid end to end along the dimension named above; an argument that names none is the same for every part. Nothing has to cross between parts.
Inputs may be any that keep to these rules, and one draw needn't show every extreme that they name: `query_ids`: each query is a run of consecutive tokens, 1 to 8 long, one of exactly 8; ids never fall. `train_ids`: each training example is a run of consecutive tokens, 1 to 16 long, one of exactly 16; ids never fall.
All inputs are finite; a program needn't handle non-finite values.
Results may differ from a plain program's by a relative error of at most 0.0049.
Values may be sent and summed in bfloat16 or wider, within the bound.
A program may use at most 256 MiB of HBM per device.

v0:
```python
import math

import jax
import jax.numpy as jnp
from jax import lax
from jax.sharding import PartitionSpec as P

QUERIES = 8
QMOST = 8
TRAIN = 16


damping_shift = 0.25


def rotate(basis, factors):
    return lax.dot_general(
        basis, factors, (((0,), (1,)), ((), ())), preferred_element_type=jnp.float32
    ).astype(jnp.bfloat16)


def query_window(query_ids):
    token_count = query_ids.shape[0]
    labels = jnp.arange(QUERIES, dtype=jnp.int32)
    starts = jnp.sum((query_ids[None, :] < labels[:, None]).astype(jnp.int32), axis=1)
    window = jnp.minimum(
        starts[:, None] + jnp.arange(QMOST, dtype=jnp.int32)[None, :], token_count - 1
    )
    live_slot = jnp.take(query_ids, window) == labels[:, None]
    return (window, live_slot)


def window_rows(columns, window):
    return jnp.transpose(jnp.take(columns, window, axis=1), (1, 2, 0))


def build_precond(left_window, right_cols, eig_cols, window):
    right_window = window_rows(right_cols, window)
    query_count = left_window.shape[0]
    group_size = math.gcd(query_count, 8)
    left_groups = left_window.reshape(
        (query_count // group_size, group_size) + left_window.shape[1:]
    )
    right_groups = right_window.reshape(
        (query_count // group_size, group_size) + right_window.shape[1:]
    )

    def one_group(operands):
        products = jnp.einsum(
            "qms,qma->qsa", operands[0], operands[1], preferred_element_type=jnp.float32
        )
        return (products / (eig_cols[None] + damping_shift)).astype(jnp.bfloat16)

    precond_groups = lax.map(one_group, (left_groups, right_groups))
    return precond_groups.reshape((query_count,) + precond_groups.shape[2:])


def on_device(
    query_grad,
    query_input,
    query_ids,
    train_grad,
    train_input,
    train_ids,
    output_basis,
    input_basis,
    eigenvalues,
):
    query_left = rotate(output_basis, query_grad)
    query_right = rotate(input_basis, query_input)
    train_left = rotate(output_basis, train_grad)
    train_right = rotate(input_basis, train_input)
    window, live_slot = query_window(query_ids)
    left_taken = window_rows(query_left, window)
    left_window = jnp.where(live_slot[:, :, None], left_taken, jnp.zeros((), jnp.bfloat16))
    right_full, train_full = (
        lax.all_gather(query_right, "mp", axis=0, tiled=True),
        lax.all_gather(train_right, "mp", axis=0, tiled=True),
    )
    precond = build_precond(left_window, right_full, eigenvalues, window)
    inner_sum = jnp.einsum("qsa,at->qst", precond, train_full, preferred_element_type=jnp.float32)
    contrib = jnp.einsum(
        "qst,st->qt", inner_sum, train_left.astype(jnp.float32), precision=lax.Precision.HIGHEST
    )
    onehot = (train_ids[:, None] == jnp.arange(TRAIN, dtype=jnp.int32)[None, :]).astype(jnp.float32)
    shares = jnp.dot(contrib, onehot, precision=lax.Precision.HIGHEST)
    return lax.psum(shares, "mp")


def solution(mesh):
    return jax.shard_map(
        on_device,
        mesh=mesh,
        in_specs=(
            P("grp", None),
            P("grp", None),
            P("grp"),
            P("grp", None),
            P("grp", None),
            P("grp"),
            P(None, "mp"),
            P(None, "mp"),
            P("mp", None),
        ),
        out_specs=P("grp", None),
        check_vma=False,
    )
```

profile of v0, /device:TPU:0, one launch (start us, length us, event | category | flops | bytes accessed | tf_op | source)
XLA Modules:
  0.0 167.1 jit_solution(38802841651659386)
XLA Ops:
  6.5 0.0 copy-start
  6.5 0.0 copy-start.1
  6.5 0.0 all-gather.2.cloned.1.call-start
  6.5 1.6 copy-done
  8.1 6.4 %convolution_convert_fusion = bf16[512,128]{1,0:T(8,128)(2,1)} fusion(bf16[8192,512]{1,0:T(8,128)(2,1)} %param.16, bf16[128,8192]{1,0:T(8,128)(2,1)S(1)} %copy-done), kind=kOutput, calls=%fused_computation.9 | convolution fusion | flops 1073807360 | bytes 10616832 | tf_op jit(solution)/shard_map/dot_general | solution.py:17
  14.5 0.0 all-gather.2.cloned.1.call-update
  14.6 0.0 copy-done.1
  14.6 0.1 convert_reduce_fusion
  14.7 0.1 compare_select_fusion
  14.8 0.1 reshape.101
  14.9 0.8 gather_fusion
  15.6 0.1 reshape.100
  15.7 0.1 iota_compare_fusion.2
  15.8 0.0 copy-done.3
  15.8 4.9 %convolution_convert_fusion.2 = bf16[512,32]{0,1:T(8,128)(2,1)S(1)} fusion(bf16[32,8192]{1,0:T(8,128)(2,1)S(1)} %copy-done.3, bf16[8192,512]{1,0:T(8,128)(2,1)} %param.16), kind=kOutput, calls=%fused_computation.13 | convolution fusion | flops 268451840 | bytes 8945664 | tf_op jit(solution)/shard_map/dot_general | solution.py:17
  20.7 24.6 %all_gather.6 = bf16[8192,32]{0,1:T(8,128)(2,1)S(1)} all-gather(bf16[512,32]{0,1:T(8,128)(2,1)S(1)} %convolution_convert_fusion.2), channel_id=1, replica_groups=mesh['grp'=2,'mp'=16] {'mp'}, dimensions={0}, use_global_device_ids=true | all-gather | bytes 557056 | tf_op jit(solution)/shard_map/all_gather | solution.py:77
  45.4 0.0 copy-start.4
  45.4 2.2 %gather_fusion.2 = bf16[64,8192]{1,0:T(8,128)(2,1)} fusion(bf16[8192,32]{0,1:T(8,128)(2,1)S(1)} %all_gather.6, s32[1024]{0:T(1024)S(1)} %pad_clamp_fusion), kind=kCustom, calls=%fused_computation.2 | custom fusion | bytes 2097408 | tf_op jit(solution)/shard_map/jit(_take)/gather | solution.py:34
  47.6 0.0 copy-done.4
  47.6 4.9 %convolution_convert_fusion.3 = bf16[512,32]{0,1:T(8,128)(2,1)S(1)} fusion(bf16[32,8192]{1,0:T(8,128)(2,1)S(1)} %copy-done.4, bf16[8192,512]{1,0:T(8,128)(2,1)} %param.15), kind=kOutput, calls=%fused_computation.14 | convolution fusion | flops 268451840 | bytes 8945664 | tf_op jit(solution)/shard_map/dot_general | solution.py:17
  52.5 0.7 gather_fusion.1
  53.2 0.0 copy-start.2
  53.2 11.9 %broadcast_add_fusion = f32[512,8192]{1,0:T(8,128)} fusion(f32[512,8192]{1,0:T(8,128)} %param.17), kind=kLoop, calls=%fused_computation.6 | loop fusion | flops 4194304 | bytes 33554432 | tf_op jit(solution)/shard_map/while/body/eval_jaxpr/add | solution.py:52
  65.1 0.0 copy-done.2
  65.1 30.2 %divide_convert_fusion.6 = bf16[8,512,8192]{2,1,0:T(8,128)(2,1)} fusion(f32[512,8192]{1,0:T(8,128)} %broadcast_add_fusion, bf16[64,8192]{1,0:T(8,128)(2,1)S(1)} %copy-done.2, pred[8,8]{1,0:T(8,128)(4,1)S(1)} %get-tuple-element.14, bf16[64,512]{1,0:T(8,128)(2,1)S(1)} %gather_fusion.1, pred[8,8]{1,0:T(8,128)(4,1)S(1)} %get-tuple-element.13), kind=kOutput, calls=%fused_computation.3.clone.clone.clone.clone.1 | convolution fusion | flops 604569600 | bytes 85000320 | tf_op jit(solution)/shard_map/while/body/eval_jaxpr/qms,qma->qsa/dot_general | solution.py:49
  95.3 6.3 %fusion.7 = f32[128,512]{0,1:T(8,128)S(1)} fusion(bf16[8192,512]{1,0:T(8,128)(2,1)} %param.15, bf16[128,8192]{1,0:T(8,128)(2,1)} %param.12), kind=kOutput, calls=%fused_computation.12 | convolution fusion | flops 1073872896 | bytes 10747904 | tf_op jit(solution)/shard_map/dot_general | solution.py:17
  101.7 0.0 copy-start.5
  101.7 0.0 all-gather.2.cloned.1.call-done
  101.7 27.9 %multiply_reduce_fusion = f32[128,8]{0,1:T(8,128)S(1)} fusion(bf16[8192,128]{1,0:T(8,128)(2,1)} %all-gather.2.cloned.1.call-done, f32[128,512]{0,1:T(8,128)S(1)} %fusion.7, bf16[8,512,8192]{2,1,0:T(8,128)(2,1)} %divide_convert_fusion.6), kind=kOutput, calls=%fused_computation.8 | convolution fusion | flops 8590982144 | bytes 69472256 | tf_op jit(solution)/shard_map/qsa,at->qst/dot_general | solution.py:81
  129.6 0.0 copy-done.5
  129.7 0.2 fusion.19
  129.8 30.4 %psum.7 = f32[8,16]{1,0:T(8,128)} all-reduce(f32[8,16]{1,0:T(8,128)S(1)} %fusion.19), channel_id=1, replica_groups=mesh['grp'=2,'mp'=16] {'mp'}, use_global_device_ids=true, to_apply=%region_1.2 | all-reduce | flops 128 | bytes 1024 | tf_op jit(solution)/shard_map/psum | solution.py:87
  (2 shorter events, 0.0 us)
Async XLA Ops:
  6.5 1.6 copy-start
  6.5 8.0 %copy-start.1 = (s32[32]{0:T(128)S(1)}, s32[32]{0:T(128)}, u32[]{:S(2)}) copy-start(s32[32]{0:T(128)} %param.11) | copy-start | bytes 388
  6.5 9.3 %copy-start.3 = (bf16[32,8192]{1,0:T(8,128)(2,1)S(1)}, bf16[32,8192]{1,0:T(8,128)(2,1)}, u32[]{:S(2)}) copy-start(bf16[32,8192]{1,0:T(8,128)(2,1)} %param.10) | copy-start | bytes 1572868
  6.5 95.2 %all-gather.2.cloned.1.call-start = ((), (), s32[]{:S(2)}) async-start(), calls=%async_computation | async-start | bytes 2228224 | tf_op jit(solution)/shard_map/all_gather | solution.py:78
  45.4 2.2 %copy-start.4 = (bf16[32,8192]{1,0:T(8,128)(2,1)S(1)}, bf16[32,8192]{1,0:T(8,128)(2,1)}, u32[]{:S(2)}) copy-start(bf16[32,8192]{1,0:T(8,128)(2,1)} %param.9) | copy-start | bytes 1572868
  53.2 11.9 %copy-start.2 = (bf16[64,8192]{1,0:T(8,128)(2,1)S(1)}, bf16[64,8192]{1,0:T(8,128)(2,1)}, u32[]{:S(2)}) copy-start(bf16[64,8192]{1,0:T(8,128)(2,1)} %gather_fusion.2) | copy-start | bytes 3145732
  101.7 28.0 %copy-start.5 = (s32[128]{0:T(128)S(1)}, s32[128]{0:T(128)}, u32[]{:S(2)}) copy-start(s32[128]{0:T(128)} %param.14) | copy-start | bytes 1540
Sparse Core Ops, SparseCore 0:
  14.7 44.4 all-gather.1
where the time goes:
time: 167 us
  matrix products  81 us (49%)
  blocking collectives  55.1 us (33%)
  between operations  13.5 us (8%)
  other arithmetic  12.1 us (7%)
  local copies, waits for them, and re-layouts  5.45 us (3%)
    psum x1, blocking collectives, on_device(): return lax.psum(shares, 'mp')  30.4 us
    dot_general x1, matrix products, one_group(): jnp.einsum('qms,qma->qsa', operands[0], operands[1], preferred_element_ty...  30.2 us
    dot_general x1, matrix products, on_device(): jnp.einsum('qsa,at->qst', precond, train_full, preferred_element_type=jnp...  27.9 us
    all_gather x1, blocking collectives, on_device(): lax.all_gather(query_right, 'mp', axis=0, tiled=True)  24.6 us
    dot_general x4, matrix products, rotate(): lax.dot_general(basis, factors, (((0,), (1,)), ((), ())), preferred_eleme...  22.6 us
    add x1, other arithmetic, one_group(): return (products / (eig_cols[None] + damping_shift)).astype(jnp.bfloat16)  11.9 us
  transfers between devices with their start and end apart: 1, of which 0 were waited for; matrix products, arithmetic and copies ran while one was open for 37% of the time, Pallas kernels for 0%

commit v1 on v0

--- a/solution.py
+++ b/solution.py
@@ -1,8 +1,11 @@
+import functools
 import math
 
 import jax
 import jax.numpy as jnp
 from jax import lax
+from jax.experimental import pallas as pl
+from jax.experimental.pallas import tpu as pltpu
 from jax.sharding import PartitionSpec as P
 
 QUERIES = 8
@@ -87,9 +90,286 @@
     return lax.psum(shares, "mp")
 
 
+Z, X, C = 4, 2, 2
+MP = Z * X * C
+CHUNKS = 8
+HALF = 256
+
+
+def scores_kernel(
+    qids_ref,
+    tids_ref,
+    qgrad,
+    qin,
+    tgrad,
+    tin,
+    obasis,
+    ibasis,
+    eig,
+    out_ref,
+    in_rows,
+    grad_rows,
+    ib,
+    ob,
+    ev,
+    inv,
+    total,
+    rights,
+    qleft,
+    tleft,
+    acc,
+    shares,
+    row_sem,
+    ib_sem,
+    ob_sem,
+    ev_sem,
+    send_sem,
+    recv_sem,
+    share_send,
+    share_recv,
+):
+    me = lax.axis_index("mp")
+    z, x, c = me // (X * C), (me // C) % X, me % C
+    qtok, depth = qin.shape
+    ttok = tin.shape[0]
+    width = ibasis.shape[1]
+    chunk = depth // CHUNKS
+
+    def z_peer(d):
+        return (z // 2 + d // 2) % 2 * 2 + (z % 2 + d % 2) % 2
+
+    def index_of(d, dx, dc):
+        return (z_peer(d) * X + (x + dx) % X) * C + (c + dc) % C
+
+    def row_copies(q, t, rows, k):
+        return (
+            pltpu.make_async_copy(q, rows.at[pl.ds(0, qtok)], row_sem.at[k]),
+            pltpu.make_async_copy(t, rows.at[pl.ds(qtok, ttok)], row_sem.at[k + 1]),
+        )
+
+    def basis_copy(source, target, sem, k):
+        part = pl.ds(pl.multiple_of(k * chunk, chunk), chunk)
+        return pltpu.make_async_copy(source.at[part], target.at[part], sem.at[k])
+
+    def block_index(i):
+        return index_of(i // 4, i % 4 // 2, i % 2)
+
+    def eig_copy(i):
+        j = block_index(i)
+        part = pl.ds(pl.multiple_of(j * width, width), width)
+        return pltpu.make_async_copy(eig.at[:, part], ev.at[j], ev_sem.at[j])
+
+    for copy in row_copies(qin, tin, in_rows, 0):
+        copy.start()
+    for k in range(CHUNKS):
+        basis_copy(ibasis, ib, ib_sem, k).start()
+    for copy in row_copies(qgrad, tgrad, grad_rows, 2):
+        copy.start()
+
+    barrier = pltpu.get_barrier_semaphore()
+
+    @pl.loop(1, MP)
+    def _(k):
+        pl.semaphore_signal(barrier, inc=1, device_id={"mp": (me + k) % MP})
+
+    def rotate_rows(rows, basis, wait_chunk):
+        total[...] = jnp.zeros_like(total)
+
+        @pl.loop(0, CHUNKS)
+        def _(k):
+            wait_chunk(k)
+            part = pl.ds(pl.multiple_of(k * chunk, chunk), chunk)
+            total[...] += jnp.dot(rows[:, part], basis[part, :], preferred_element_type=jnp.float32)
+
+    def wait_in(k):
+        basis_copy(ibasis, ib, ib_sem, k).wait()
+        basis_copy(obasis, ob, ob_sem, k).start()
+
+    def wait_out(k):
+        basis_copy(obasis, ob, ob_sem, k).wait()
+        eig_copy(2 * k).start()
+        eig_copy(2 * k + 1).start()
+
+    for copy in row_copies(qin, tin, in_rows, 0):
+        copy.wait()
+    rotate_rows(in_rows, ib, wait_in)
+    rights[me] = total[...].astype(jnp.bfloat16)
+
+    pl.semaphore_wait(barrier, MP - 1)
+
+    def send(j, peer, kind, d):
+        return pltpu.make_async_remote_copy(
+            src_ref=rights.at[j],
+            dst_ref=rights.at[j],
+            send_sem=send_sem.at[kind, d],
+            recv_sem=recv_sem.at[j],
+            device_id={"mp": peer},
+        )
+
+    x_peer, core_peer = index_of(0, 1, 0), index_of(0, 0, 1)
+    send(me, core_peer, 2, 0).start()
+    send(me, x_peer, 1, 0).start()
+    for d in range(1, Z):
+        send(me, index_of(d, 0, 0), 0, d).start()
+
+    for copy in row_copies(qgrad, tgrad, grad_rows, 2):
+        copy.wait()
+    rotate_rows(grad_rows, ob, wait_out)
+    tleft[...] = total[pl.ds(qtok, ttok), :].astype(jnp.bfloat16)
+    turned = total[pl.ds(0, 128), :].astype(jnp.bfloat16).astype(jnp.float32).T[:, :qtok]
+    qids = qids_ref[...]
+    last = lax.broadcasted_iota(jnp.int32, (1, qtok), 1) == qtok - 1
+    for q in range(QUERIES):
+        start = jnp.sum(jnp.where(qids < q, 1.0, 0.0), axis=1, keepdims=True)
+        repeats = jnp.where(last, start + (QMOST - qtok + 1), 1.0)
+        weights = jnp.where(qids == q, repeats, 0.0)
+        qleft[q] = (turned * weights).astype(jnp.bfloat16)
+    acc[...] = jnp.zeros_like(acc)
+
+    def arrived(j):
+        send(j, core_peer, 0, 0).wait_recv()
+
+    @pl.loop(0, MP)
+    def _(i):
+        d, r = i // 4, i % 4
+        j = block_index(i)
+
+        @pl.when(jnp.logical_and(r == 2, d < Z - 1))
+        def _():
+            nearer = index_of(d + 1, 0, 0)
+            arrived(nearer)
+            send(nearer, x_peer, 1, d + 1).start()
+            send(nearer, core_peer, 2, d + 1).start()
+
+        @pl.when(r == 1)
+        def _():
+            arrived(j)
+            across = index_of(d, 1, 0)
+            arrived(across)
+            send(across, core_peer, 3, d).start()
+
+        @pl.when(r == 3)
+        def _():
+            arrived(j)
+
+        eig_copy(i).wait()
+        inv[...] = 1.0 / (ev[j] + damping_shift)
+
+        @pl.loop(0, QUERIES, unroll=UNROLL)
+        def _(q):
+            for h in range(0, width, HALF):
+                part = pl.ds(h, HALF)
+                products = jnp.dot(
+                    qleft[q], rights[j, pl.ds(0, qtok), part], preferred_element_type=jnp.float32
+                )
+                precond = (products * inv[:, part]).astype(jnp.bfloat16)
+                inner = jnp.dot(tleft[...], precond, preferred_element_type=jnp.float32)
+                inner = inner * rights[j, pl.ds(qtok, ttok), part].astype(jnp.float32)
+                folded = inner[:, :128]
+                for lane in range(128, HALF, 128):
+                    folded = folded + inner[:, lane : lane + 128]
+                acc[q] += folded
+
+    lanes = lax.broadcasted_iota(jnp.int32, (ttok, 128), 1)
+    contrib = jnp.zeros((ttok, 128), jnp.float32)
+    for q in range(QUERIES):
+        contrib = jnp.where(lanes == q, jnp.sum(acc[q], axis=1, keepdims=True), contrib)
+    labels = lax.broadcasted_iota(jnp.int32, (128, ttok), 0)
+    onehot = jnp.where(labels == tids_ref[...], 1.0, 0.0)
+    shares[me] = lax.dot_general(
+        contrib.T[:QUERIES],
+        onehot,
+        (((1,), (1,)), ((), ())),
+        precision=lax.Precision.HIGHEST,
+        preferred_element_type=jnp.float32,
+    )
+
+    def share_copy(k, j):
+        return pltpu.make_async_remote_copy(
+            src_ref=shares.at[j],
+            dst_ref=shares.at[j],
+            send_sem=share_send.at[k],
+            recv_sem=share_recv.at[j],
+            device_id={"mp": (me + k) % MP},
+        )
+
+    @pl.loop(1, MP)
+    def _(k):
+        share_copy(k, me).start()
+
+    for d in range(Z):
+        if d > 0:
+            send(me, index_of(d, 0, 0), 0, d).wait_send()
+        send(me, x_peer, 1, d).wait_send()
+        send(me, core_peer, 2, d).wait_send()
+        send(me, core_peer, 3, d).wait_send()
+
+    @pl.loop(1, MP)
+    def _(k):
+        share_copy(k, (me + k) % MP).wait_recv()
+
+    @pl.loop(1, MP)
+    def _(k):
+        share_copy(k, me).wait_send()
+
+    result = shares[0]
+    for j in range(1, MP):
+        result = result + shares[j]
+    out_ref[...] = result[:, :TRAIN]
+
+
+UNROLL = 4
+
+
+def fused_scores(qgrad, qin, qids, tgrad, tin, tids, obasis, ibasis, eig):
+    qtok, depth = qin.shape
+    ttok = tin.shape[0]
+    width = ibasis.shape[1]
+    tokens = qtok + ttok
+    vmem = pl.BlockSpec(memory_space=pltpu.VMEM)
+    hbm = pl.BlockSpec(memory_space=pl.ANY)
+    dma = pltpu.SemaphoreType.DMA
+    return pl.pallas_call(
+        scores_kernel,
+        out_shape=jax.ShapeDtypeStruct((QUERIES, TRAIN), jnp.float32),
+        in_specs=[vmem, vmem] + [hbm] * 7,
+        out_specs=vmem,
+        scratch_shapes=[
+            pltpu.VMEM((tokens, depth), jnp.bfloat16),
+            pltpu.VMEM((tokens, depth), jnp.bfloat16),
+            pltpu.VMEM((depth, width), jnp.bfloat16),
+            pltpu.VMEM((depth, width), jnp.bfloat16),
+            pltpu.VMEM((MP, width, width), jnp.float32),
+            pltpu.VMEM((width, width), jnp.float32),
+            pltpu.VMEM((tokens, width), jnp.float32),
+            pltpu.VMEM((MP, tokens, width), jnp.bfloat16),
+            pltpu.VMEM((QUERIES, width, qtok), jnp.bfloat16),
+            pltpu.VMEM((ttok, width), jnp.bfloat16),
+            pltpu.VMEM((QUERIES, ttok, 128), jnp.float32),
+            pltpu.VMEM((MP, QUERIES, 128), jnp.float32),
+            dma((4,)),
+            dma((CHUNKS,)),
+            dma((CHUNKS,)),
+            dma((MP,)),
+            dma((4, Z)),
+            dma((MP,)),
+            dma((MP,)),
+            dma((MP,)),
+        ],
+        compiler_params=pltpu.CompilerParams(
+            collective_id=0, has_side_effects=True, vmem_limit_bytes=56 * 2**20
+        ),
+    )(qids.reshape(1, qtok), tids.reshape(1, ttok), qgrad, qin, tgrad, tin, obasis, ibasis, eig)
+
+
+def device_part(mp, qgrad, qin, qids, tgrad, tin, tids, obasis, ibasis, eig):
+    run = fused_scores if mp == MP else on_device
+    return run(qgrad, qin, qids, tgrad, tin, tids, obasis, ibasis, eig)
+
+
 def solution(mesh):
     return jax.shard_map(
-        on_device,
+        functools.partial(device_part, mesh.shape["mp"]),
         mesh=mesh,
         in_specs=(
             P("grp", None),

time: 167 us -> 103 us (0.62)
  Pallas kernels: 0 us -> 101 us
  matrix products: 81 us -> 0 us
  blocking collectives: 55.1 us -> 0 us
  between operations: 13.5 us -> 0.01 us
  other arithmetic: 12.1 us -> 0 us
  local copies, waits for them, and re-layouts: 5.45 us -> 1.28 us
    pallas_call x0 -> x1, Pallas kernels: none -> 101 us  [fused_scores(): pl.pallas_call(scores_kernel, out_shape=jax.ShapeDtypeStruct((QUERIES, TR...]
    dot_general x7 -> x0, matrix products: 81 us -> none  [the longest x1 30.2 us: one_group(): jnp.einsum('qms,qma->qsa', operands[0], operands[1], preferred_element_ty...]
    psum x1 -> x0, blocking collectives: 30.4 us -> none  [on_device(): return lax.psum(shares, 'mp')]
    all_gather x1 -> x0, blocking collectives: 24.6 us -> none  [on_device(): lax.all_gather(query_right, 'mp', axis=0, tiled=True)]
    add x1 -> x0, other arithmetic: 11.9 us -> none  [one_group(): return (products / (eig_cols[None] + damping_shift)).astype(jnp.bfloat16)]
    gather x4 -> x0, local copies, waits for them, and re-layouts: 3.76 us -> none  [the longest x2 2.9 us: window_rows(): return jnp.transpose(jnp.take(columns, window, axis=1), (1, 2, 0))]
  transfers between devices with their start and end apart: 1 -> 0, of which waited for: 0 -> 0; matrix products, arithmetic and copies ran while one was open for 37% -> 0% of each run, Pallas kernels for 0% -> 0%
where the time goes in v1:
time: 103 us; the launch traced here: 102 us
  Pallas kernels  101 us (98%)
  local copies, waits for them, and re-layouts  1.28 us (1%)
    pallas_call x1, Pallas kernels, fused_scores(): pl.pallas_call(scores_kernel, out_shape=jax.ShapeDtypeStruct((QUERIES, TR...  101 us

profile of v1, /device:TPU:0, one launch (start us, length us, event | category | flops | bytes accessed | tf_op | source)
XLA Modules:
  0.0 102.3 jit_solution(6580351969348096863)
XLA Ops:
  0.0 101.1 %shard_map.91 = f32[8,16]{1,0:T(8,128)} custom-call(s32[1,32]{1,0:T(1,128)} %bitcast.2, s32[1,128]{1,0:T(1,128)} %bitcast.3, bf16[32,8192]{1,0:T(8,128)(2,1)} %qgrad.1, bf16[32,8192]{1,0:T(8,128)(2,1)} %qin.1, bf16[128,8192]{1,0:T(8,128)(2,1)} %tgrad.1, bf16[128,8192]{1,0:T(8,128)(2,1)} %tin.1, bf16[8192,512]{1,0:T(8,128)(2,1)} %obasis.1, ...), custom_call_target="tpu_custom_call" | custom-call | tf_op jit(solution)/shard_map/pallas_call | solution.py:332
  101.1 1.3 %copy.11 = f32[8,16]{1,0:T(8,128)} copy(f32[8,16]{1,0:T(8,128)} %shard_map.91) | data formatting | bytes 1024

commit v2 on v1

--- a/solution.py
+++ b/solution.py
@@ -93,7 +93,6 @@
 Z, X, C = 4, 2, 2
 MP = Z * X * C
 CHUNKS = 8
-HALF = 256
 
 
 def scores_kernel(
@@ -113,6 +112,7 @@
     ob,
     ev,
     inv,
+    precond,
     total,
     rights,
     qleft,
@@ -255,20 +255,25 @@
         eig_copy(i).wait()
         inv[...] = 1.0 / (ev[j] + damping_shift)
 
-        @pl.loop(0, QUERIES, unroll=UNROLL)
-        def _(q):
-            for h in range(0, width, HALF):
-                part = pl.ds(h, HALF)
-                products = jnp.dot(
-                    qleft[q], rights[j, pl.ds(0, qtok), part], preferred_element_type=jnp.float32
-                )
-                precond = (products * inv[:, part]).astype(jnp.bfloat16)
-                inner = jnp.dot(tleft[...], precond, preferred_element_type=jnp.float32)
-                inner = inner * rights[j, pl.ds(qtok, ttok), part].astype(jnp.float32)
-                folded = inner[:, :128]
-                for lane in range(128, HALF, 128):
-                    folded = folded + inner[:, lane : lane + 128]
-                acc[q] += folded
+        def form(q):
+            products = jnp.dot(
+                qleft[q], rights[j, pl.ds(0, qtok)], preferred_element_type=jnp.float32
+            )
+            precond[q % 2] = (products * inv[...]).astype(jnp.bfloat16)
+
+        def contract(q):
+            inner = jnp.dot(tleft[...], precond[q % 2], preferred_element_type=jnp.float32)
+            inner = inner * rights[j, pl.ds(qtok, ttok)].astype(jnp.float32)
+            folded = inner[:, :128]
+            for lane in range(128, width, 128):
+                folded = folded + inner[:, lane : lane + 128]
+            acc[q] += folded
+
+        form(0)
+        for q in range(1, QUERIES):
+            form(q)
+            contract(q - 1)
+        contract(QUERIES - 1)
 
     lanes = lax.broadcasted_iota(jnp.int32, (ttok, 128), 1)
     contrib = jnp.zeros((ttok, 128), jnp.float32)
@@ -316,9 +321,6 @@
     for j in range(1, MP):
         result = result + shares[j]
     out_ref[...] = result[:, :TRAIN]
-
-
-UNROLL = 4
 
 
 def fused_scores(qgrad, qin, qids, tgrad, tin, tids, obasis, ibasis, eig):
@@ -341,6 +343,7 @@
             pltpu.VMEM((depth, width), jnp.bfloat16),
             pltpu.VMEM((MP, width, width), jnp.float32),
             pltpu.VMEM((width, width), jnp.float32),
+            pltpu.VMEM((2, width, width), jnp.bfloat16),
             pltpu.VMEM((tokens, width), jnp.float32),
             pltpu.VMEM((MP, tokens, width), jnp.bfloat16),
             pltpu.VMEM((QUERIES, width, qtok), jnp.bfloat16),

time: 103 us -> 52.2 us (0.51)
  Pallas kernels: 101 us -> 50.8 us
    pallas_call x1, Pallas kernels: 101 us -> 50.8 us  [fused_scores(): pl.pallas_call(scores_kernel, out_shape=jax.ShapeDtypeStruct((QUERIES, TR...]
where the time goes in v2:
time: 52.2 us; the launch traced here: 52.1 us
  Pallas kernels  50.8 us (97%)
  local copies, waits for them, and re-layouts  1.28 us (2%)
    pallas_call x1, Pallas kernels, fused_scores(): pl.pallas_call(scores_kernel, out_shape=jax.ShapeDtypeStruct((QUERIES, TR...  50.8 us
    unnamed x1, local copies, waits for them, and re-layouts  1.28 us

profile of v2, /device:TPU:0, one launch (start us, length us, event | category | flops | bytes accessed | tf_op | source)
XLA Modules:
  0.0 52.1 jit_solution(13314857880682714544)
XLA Ops:
  0.0 50.8 %shard_map.91 = f32[8,16]{1,0:T(8,128)} custom-call(s32[1,32]{1,0:T(1,128)} %bitcast.2, s32[1,128]{1,0:T(1,128)} %bitcast.3, bf16[32,8192]{1,0:T(8,128)(2,1)} %qgrad.1, bf16[32,8192]{1,0:T(8,128)(2,1)} %qin.1, bf16[128,8192]{1,0:T(8,128)(2,1)} %tgrad.1, bf16[128,8192]{1,0:T(8,128)(2,1)} %tin.1, bf16[8192,512]{1,0:T(8,128)(2,1)} %obasis.1, ...), custom_call_target="tpu_custom_call" | custom-call | tf_op jit(solution)/shard_map/pallas_call | solution.py:334
  50.8 1.3 %copy.11 = f32[8,16]{1,0:T(8,128)} copy(f32[8,16]{1,0:T(8,128)} %shard_map.91) | data formatting | bytes 1024

commit v3 on v2

--- a/solution.py
+++ b/solution.py
@@ -135,11 +135,17 @@
     width = ibasis.shape[1]
     chunk = depth // CHUNKS
 
-    def z_peer(d):
-        return (z // 2 + d // 2) % 2 * 2 + (z % 2 + d % 2) % 2
-
-    def index_of(d, dx, dc):
-        return (z_peer(d) * X + (x + dx) % X) * C + (c + dc) % C
+    upper, inner_z = z // 2, (z + 1) // 2 % 2
+
+    def z_source(k):
+        place = k + inner_z * (1 - 2 * (k % 2)) * (1 - k // 2)
+        return place * (1 - 2 * upper) + (Z - 1) * upper
+
+    def index_at(at_z, dx, dc):
+        return (at_z * X + (x + dx) % X) * C + (c + dc) % C
+
+    def index_of(k, dx, dc):
+        return index_at(z_source(k), dx, dc)
 
     def row_copies(q, t, rows, k):
         return (
@@ -209,8 +215,14 @@
     x_peer, core_peer = index_of(0, 1, 0), index_of(0, 0, 1)
     send(me, core_peer, 2, 0).start()
     send(me, x_peer, 1, 0).start()
-    for d in range(1, Z):
-        send(me, index_of(d, 0, 0), 0, d).start()
+
+    @pl.when(z < Z - 1)
+    def _():
+        send(me, index_at(z + 1, 0, 0), 0, 0).start()
+
+    @pl.when(z > 0)
+    def _():
+        send(me, index_at(z - 1, 0, 0), 4, 0).start()
 
     for copy in row_copies(qgrad, tgrad, grad_rows, 2):
         copy.wait()
@@ -234,12 +246,27 @@
         d, r = i // 4, i % 4
         j = block_index(i)
 
-        @pl.when(jnp.logical_and(r == 2, d < Z - 1))
-        def _():
-            nearer = index_of(d + 1, 0, 0)
-            arrived(nearer)
-            send(nearer, x_peer, 1, d + 1).start()
-            send(nearer, core_peer, 2, d + 1).start()
+        def pass_on(k):
+            source_z = z_source(k)
+            block = index_at(source_z, 0, 0)
+            arrived(block)
+
+            @pl.when(jnp.logical_and(inner_z == 1, source_z < z))
+            def _():
+                send(block, index_at(z + 1, 0, 0), 0, k).start()
+
+            @pl.when(jnp.logical_and(inner_z == 1, source_z > z))
+            def _():
+                send(block, index_at(z - 1, 0, 0), 0, k).start()
+
+            send(block, x_peer, 1, k).start()
+            send(block, core_peer, 2, k).start()
+
+        for k in range(1, Z):
+
+            @pl.when(i == 2 * (k - 1) - inner_z * ((k - 1) * 2 - k // 3 * 2))
+            def _():
+                pass_on(k)
 
         @pl.when(r == 1)
         def _():
@@ -302,9 +329,21 @@
     def _(k):
         share_copy(k, me).start()
 
+    @pl.when(z < Z - 1)
+    def _():
+        send(me, core_peer, 0, 0).wait_send()
+
+    @pl.when(z > 0)
+    def _():
+        send(me, core_peer, 4, 0).wait_send()
+
     for d in range(Z):
         if d > 0:
-            send(me, index_of(d, 0, 0), 0, d).wait_send()
+
+            @pl.when(inner_z == 1)
+            def _():
+                send(me, core_peer, 0, d).wait_send()
+
         send(me, x_peer, 1, d).wait_send()
         send(me, core_peer, 2, d).wait_send()
         send(me, core_peer, 3, d).wait_send()
@@ -354,7 +393,7 @@
             dma((CHUNKS,)),
             dma((CHUNKS,)),
             dma((MP,)),
-            dma((4, Z)),
+            dma((5, Z)),
             dma((MP,)),
             dma((MP,)),
             dma((MP,)),

time: 52.2 us -> 55.1 us (1.056)
  Pallas kernels: 50.8 us -> 53.6 us
    pallas_call x1, Pallas kernels: 50.8 us -> 53.6 us  [fused_scores(): pl.pallas_call(scores_kernel, out_shape=jax.ShapeDtypeStruct((QUERIES, TR...]
where the time goes in v3:
time: 55.1 us; the launch traced here: 54.9 us
  Pallas kernels  53.6 us (97%)
  local copies, waits for them, and re-layouts  1.28 us (2%)
    pallas_call x1, Pallas kernels, fused_scores(): pl.pallas_call(scores_kernel, out_shape=jax.ShapeDtypeStruct((QUERIES, TR...  53.6 us
    unnamed x1, local copies, waits for them, and re-layouts  1.28 us

profile of v3, /device:TPU:0, one launch (start us, length us, event | category | flops | bytes accessed | tf_op | source)
XLA Modules:
  0.0 54.9 jit_solution(16424662273219185827)
XLA Ops:
  0.0 53.6 %shard_map.91 = f32[8,16]{1,0:T(8,128)} custom-call(s32[1,32]{1,0:T(1,128)} %bitcast.2, s32[1,128]{1,0:T(1,128)} %bitcast.3, bf16[32,8192]{1,0:T(8,128)(2,1)} %qgrad.1, bf16[32,8192]{1,0:T(8,128)(2,1)} %qin.1, bf16[128,8192]{1,0:T(8,128)(2,1)} %tgrad.1, bf16[128,8192]{1,0:T(8,128)(2,1)} %tin.1, bf16[8192,512]{1,0:T(8,128)(2,1)} %obasis.1, ...), custom_call_target="tpu_custom_call" | custom-call | tf_op jit(solution)/shard_map/pallas_call | solution.py:373
  53.6 1.3 %copy.11 = f32[8,16]{1,0:T(8,128)} copy(f32[8,16]{1,0:T(8,128)} %shard_map.91) | data formatting | bytes 1024

commit v4 on v3

--- a/solution.py
+++ b/solution.py
@@ -264,7 +264,7 @@
 
         for k in range(1, Z):
 
-            @pl.when(i == 2 * (k - 1) - inner_z * ((k - 1) * 2 - k // 3 * 2))
+            @pl.when(i == 4 * k - 3 - inner_z * (0, 0, 3, 4)[k])
             def _():
                 pass_on(k)
 

time: 55.1 us -> 52.4 us (0.951)
  Pallas kernels: 53.6 us -> 50.9 us
    pallas_call x1, Pallas kernels: 53.6 us -> 50.9 us  [fused_scores(): pl.pallas_call(scores_kernel, out_shape=jax.ShapeDtypeStruct((QUERIES, TR...]
where the time goes in v4:
time: 52.4 us; the launch traced here: 52.2 us
  Pallas kernels  50.9 us (97%)
  local copies, waits for them, and re-layouts  1.28 us (2%)
    pallas_call x1, Pallas kernels, fused_scores(): pl.pallas_call(scores_kernel, out_shape=jax.ShapeDtypeStruct((QUERIES, TR...  50.9 us
    unnamed x1, local copies, waits for them, and re-layouts  1.28 us

profile of v4, /device:TPU:0, one launch (start us, length us, event | category | flops | bytes accessed | tf_op | source)
XLA Modules:
  0.0 52.2 jit_solution(4953956863172803820)
XLA Ops:
  0.0 50.9 %shard_map.91 = f32[8,16]{1,0:T(8,128)} custom-call(s32[1,32]{1,0:T(1,128)} %bitcast.2, s32[1,128]{1,0:T(1,128)} %bitcast.3, bf16[32,8192]{1,0:T(8,128)(2,1)} %qgrad.1, bf16[32,8192]{1,0:T(8,128)(2,1)} %qin.1, bf16[128,8192]{1,0:T(8,128)(2,1)} %tgrad.1, bf16[128,8192]{1,0:T(8,128)(2,1)} %tin.1, bf16[8192,512]{1,0:T(8,128)(2,1)} %obasis.1, ...), custom_call_target="tpu_custom_call" | custom-call | tf_op jit(solution)/shard_map/pallas_call | solution.py:373
  51.0 1.3 %copy.11 = f32[8,16]{1,0:T(8,128)} copy(f32[8,16]{1,0:T(8,128)} %shard_map.91) | data formatting | bytes 1024
